TPU v7x, 256 devices: a whole 4x4x8 slice. The times are simulated.
256 devices in a mesh: dp: 32 (over x, z_hi, core), ctx: 8 (over y, z_lo).
Axes of the slice: x: 4, y: 4, z: 8 (z_hi: 4, z_lo: 2; z = z_hi * 2 + z_lo), core: 2. Of those that a mesh axis runs over, the one named last changes fastest.
Arguments:
- query: bfloat16 [65536, 4096], P(('dp', 'ctx'))
- keys: bfloat16 [65536, 512], P(('dp', 'ctx'))
- values: bfloat16 [65536, 512], P(('dp', 'ctx')), may hold values from -6 to 6
- segments: int32 [65536], P(('dp', 'ctx')), may hold values from 0 to 3, as said below
Outputs:
- attended: bfloat16 [65536, 4096], P(('dp', 'ctx'))
Inputs may be any that keep to these rules, and one draw needn't show every extreme that they name: `segments`: constant over aligned blocks of 128 tokens; within each window of 2048 tokens the numbers start at 0 and rise by one at each document start, so a window holds 1 to 4 documents; some window holds 4.
All inputs are finite; a program needn't handle non-finite values.
Results may differ from a plain program's by a relative error of at most 0.0039.
Values may be sent and summed in bfloat16 or wider, within the bound.
No kernel may reach another device: no remote copies, remote signals or barrier semaphores. Data moves between devices by JAX's collectives and lax.ppermute only.
A program may use at most 64 MiB of HBM per device.

v0:
```python
import math

import jax
import jax.numpy as jnp
from jax import lax
from jax.sharding import PartitionSpec as P

QH = 32
KVH = 4
HD = 128


masked_score = -1e30


def swapped(value, axis, bit):
    mask = 2**bit
    pairs = [(source, source ^ mask) for source in range(lax.axis_size(axis))]
    return lax.ppermute(value, axis, pairs)


def key_block(state, heads_q, query_pos, query_seg, key_rows, value_rows, key_seg, key_pos):
    allowed = (query_seg[:, None] == key_seg[None, :]) & (key_pos[None, :] <= query_pos[:, None])

    def compute(current):
        row_top, totals, weighted = current
        kv_groups = heads_q.shape[1]
        key_count = key_rows.shape[0]
        heads_k = key_rows.reshape(key_count, kv_groups, HD)
        heads_v = value_rows.reshape(key_count, kv_groups, HD)
        scores = jnp.einsum(
            "rgjd,lgd->gjrl", heads_q, heads_k, preferred_element_type=jnp.float32
        ) * HD ** (-0.5)
        scores = jnp.where(allowed, scores, masked_score)
        new_top = jnp.maximum(row_top, jnp.max(scores, axis=-1))
        weights = jnp.where(allowed, jnp.exp(scores - new_top[..., None]), 0.0)
        rescale = jnp.exp(row_top - new_top)
        totals = totals * rescale + jnp.sum(weights, axis=-1)
        weighted = weighted * rescale[..., None] + jnp.einsum(
            "gjrl,lgd->gjrd",
            weights.astype(jnp.bfloat16),
            heads_v,
            preferred_element_type=jnp.float32,
        )
        return (new_top, totals, weighted)

    def unchanged(current):
        return current

    return lax.cond(jnp.any(allowed), compute, unchanged, state)


def sweep(state, heads_q, query_pos, query_seg, key_rows, value_rows, key_seg, anchor):
    key_count = key_rows.shape[0]
    block_width = math.gcd(key_count, 512)

    def advance(step_index, current):
        offset = step_index * block_width
        return key_block(
            current,
            heads_q,
            query_pos,
            query_seg,
            lax.dynamic_slice_in_dim(key_rows, offset, block_width, 0),
            lax.dynamic_slice_in_dim(value_rows, offset, block_width, 0),
            lax.dynamic_slice_in_dim(key_seg, offset, block_width, 0),
            anchor + offset + jnp.arange(block_width),
        )

    return lax.fori_loop(0, key_count // block_width, advance, state)


def empty_state(row_count, kv_groups):
    state_shape = (kv_groups, QH // KVH, row_count)
    return (
        jnp.full(state_shape, masked_score, jnp.float32),
        jnp.zeros(state_shape, jnp.float32),
        jnp.zeros(state_shape + (HD,), jnp.float32),
    )


def finish(state):
    row_top, totals, weighted = state
    merged = weighted / totals[..., None]
    kv_groups, per_group, row_count, head_size = merged.shape
    return (
        merged.transpose(2, 0, 1, 3)
        .reshape(row_count, kv_groups * per_group * head_size)
        .astype(jnp.bfloat16)
    )


def split_heads(query_rows, kv_groups):
    return query_rows.reshape(query_rows.shape[0], kv_groups, QH // KVH, HD)


def columns(block, block_width, side):
    return lax.dynamic_slice_in_dim(block, side * block_width, block_width, 1)


def local(query, keys, values, segments):
    row_count = query.shape[0]
    ctx_place = lax.axis_index("ctx")
    query_pos = ctx_place * row_count + jnp.arange(row_count)
    half_q = QH // 2 * HD
    half_kv = KVH // 2 * HD
    pair_bit = 0
    high_side = lax.axis_index("dp") >> pair_bit & 1
    low_side = 1 - high_side
    own_heads = split_heads(columns(query, half_q, high_side), KVH // 2)
    key_rows, value_rows, seg_rows = (
        lax.all_gather(keys, "ctx", axis=0, tiled=True),
        lax.all_gather(values, "ctx", axis=0, tiled=True),
        lax.all_gather(segments, "ctx", axis=0, tiled=True),
    )
    got_q, got_k, got_v, got_seg = swapped(
        (
            columns(query, half_q, low_side),
            columns(key_rows, half_kv, low_side),
            columns(value_rows, half_kv, low_side),
            seg_rows,
        ),
        "dp",
        pair_bit,
    )
    partner_seg = jnp.take(got_seg, query_pos, axis=0)
    own_state = sweep(
        empty_state(row_count, KVH // 2),
        own_heads,
        query_pos,
        segments,
        columns(key_rows, half_kv, high_side),
        columns(value_rows, half_kv, high_side),
        seg_rows,
        0,
    )
    their_state = sweep(
        empty_state(row_count, KVH // 2),
        split_heads(got_q, KVH // 2),
        query_pos,
        partner_seg,
        got_k,
        got_v,
        got_seg,
        0,
    )
    returned = swapped(finish(their_state), "dp", pair_bit)
    own_out = finish(own_state)
    result = jnp.where(
        high_side == 0,
        jnp.concatenate([own_out, returned], axis=1),
        jnp.concatenate([returned, own_out], axis=1),
    )
    return result


def solution(mesh):
    placed = (
        P(("dp", "ctx"), None),
        P(("dp", "ctx"), None),
        P(("dp", "ctx"), None),
        P(("dp", "ctx")),
    )
    return jax.shard_map(
        local, mesh=mesh, in_specs=placed, out_specs=P(("dp", "ctx"), None), check_vma=False
    )
```

profile of v0, /device:TPU:31, one launch (start us, length us, event | category | flops | bytes accessed | tf_op | source)
XLA Modules:
  0.0 246.2 jit_solution(12436194385707393867)
XLA Ops:
  6.5 1.8 copy.29
  8.4 1.8 copy.31
  10.2 1.7 constant_dynamic-slice_fusion.8
  11.9 1.3 copy.52
  13.9 49.6 %all-gather.4.cloned.1.call-done = bf16[2048,512]{0,1:T(8,128)(2,1)} async-done(((bf16[256,512]{0,1:T(8,128)(2,1)}), bf16[2048,512]{0,1:T(8,128)(2,1)}) %all-gather.4.cloned.1.call-update) | async-done | bytes 2097168 | tf_op jit(solution)/shard_map/all_gather | solution.py:112
  63.6 3.1 %constant_dynamic-slice_fusion.9 = (bf16[2048,256]{0,1:T(8,128)(2,1)}, bf16[2048,256]{0,1:T(8,128)(2,1)}) fusion(bf16[2048,512]{0,1:T(8,128)(2,1)} %all-gather.4.cloned.1.call-done, s32[]{:T(128)S(6)} %select_n.82, s32[]{:T(128)S(6)} %select_n.87), kind=kLoop, calls=%fused_computation.55 | loop fusion | bytes 4194312 | tf_op jit(solution)/shard_map/dynamic_slice | solution.py:98
  66.7 3.0 %collective-permute-start.1 = (bf16[2048,256]{0,1:T(8,128)(2,1)}, bf16[2048,256]{0,1:T(8,128)(2,1)S(1)}, u32[]{:S(2)}, u32[]{:S(2)}) collective-permute-start(bf16[2048,256]{0,1:T(8,128)(2,1)} %get-tuple-element.662), channel_id=1, source_target_pairs={{0,8},{8,0},{16,24},{24,16},{32,40},{40,32},{48,56},{56,48},{64,72... | collective-permute-start | bytes 3145736 | tf_op jit(solution)/shard_map/ppermute | solution.py:19
  69.7 49.8 %all-gather.6.cloned.1.call-done = bf16[2048,512]{0,1:T(8,128)(2,1)} async-done(((bf16[256,512]{0,1:T(8,128)(2,1)}), bf16[2048,512]{0,1:T(8,128)(2,1)}) %all-gather.6.cloned.1.call-update) | async-done | bytes 2097168 | tf_op jit(solution)/shard_map/all_gather | solution.py:113
  119.5 3.2 %constant_dynamic-slice_fusion.7 = (bf16[2048,256]{0,1:T(8,128)(2,1)}, bf16[2048,256]{0,1:T(8,128)(2,1)}) fusion(bf16[2048,512]{0,1:T(8,128)(2,1)} %all-gather.6.cloned.1.call-done, s32[]{:T(128)S(6)} %select_n.82, s32[]{:T(128)S(6)} %select_n.87), kind=kLoop, calls=%fused_computation.53 | loop fusion | bytes 4194312 | tf_op jit(solution)/shard_map/dynamic_slice | solution.py:98
  122.7 3.0 %collective-permute-start.3 = (bf16[2048,256]{0,1:T(8,128)(2,1)}, bf16[2048,256]{0,1:T(8,128)(2,1)}, u32[]{:S(2)}, u32[]{:S(2)}) collective-permute-start(bf16[2048,256]{0,1:T(8,128)(2,1)} %get-tuple-element.658), channel_id=1, source_target_pairs={{0,8},{8,0},{16,24},{24,16},{32,40},{40,32},{48,56},{56,48},{64,72... | collective-permute-start | bytes 3145736 | tf_op jit(solution)/shard_map/ppermute | solution.py:19
  125.6 11.5 %all-gather = s32[8,1,256]{2,1,0:T(1,128)S(1)} all-gather(s32[1,1,256]{2,1,0:T(1,128)S(1)} %bitcast.81), channel_id=1, replica_groups=mesh['dp'=32,'ctx'=8] {'ctx'}, dimensions={0}, use_global_device_ids=true | all-gather | bytes 9216 | tf_op jit(solution)/shard_map/all_gather | solution.py:114
  137.2 3.5 %collective-permute-start = (s32[2048]{0:T(1024)S(1)}, s32[2048]{0:T(1024)S(1)}, u32[]{:S(2)}, u32[]{:S(2)}) collective-permute-start(s32[2048]{0:T(1024)S(1)} %bitcast.79), channel_id=1, source_target_pairs={{0,8},{8,0},{16,24},{24,16},{32,40},{40,32},{48,56},{56,48},{64,72... | collective-permute-start | bytes 24584 | tf_op jit(solution)/shard_map/ppermute | solution.py:19
  141.9 1.7 gather_fusion
  143.6 1.6 copy.35
  145.3 1.5 broadcast.82.clone
  146.8 43.6 %while.37 = (s32[]{:T(128)}, f32[2,8,256]{2,1,0:T(8,128)S(1)}, f32[2,8,256]{2,1,0:T(8,128)S(1)}, f32[2,8,256,128]{3,2,1,0:T(8,128)}, s32[256]{0:T(256)S(1)}, /*i...) while((s32[]{:T(128)}, f32[2,8,256]{2,1,0:T(8,128)S(1)}, ...), condition=%wide.region_13.14_spmd.clone, body=%wide.region_7.13_spmd.clone.sunk | while | flops 1102586624 | bytes 49558904 | solution.py:70
  148.3 9.4 %conditional.7 = ((f32[2,8,256]{2,1,0:T(8,128)S(1)}, f32[2,8,256]{2,1,0:T(8,128)S(1)}, f32[2,8,256,128]{3,2,1,0:T(8,128)})) conditional(s32[]{:T(128)} %convert_element_type.67, (f32[2,8,256]{2,1,0:T(8,128)S(1)}, f32[2,8,256]{2,1,0:T(8,128)S(1)}, f32[2,8,256,128]{3,2,1,0:T(8,128)}) %tuple.108, (pred[256,512]{0,1:T(8,128)(4,1)S(1)}, ...), branch_computations={%region_9.9_spmd, %region_10.12_spmd} | conditional | flops 1102061568 | bytes 49414236 | solution.py:50
  148.3 1.0 constant_dynamic-slice_fusion.2
  149.3 1.5 fusion.15
  150.9 2.0 fusion.17
  152.9 3.5 %multiply_add_fusion.2 = f32[2,8,256,128]{3,2,1,0:T(8,128)S(1)} fusion(f32[2,8,256,128]{3,2,1,0:T(8,128)S(1)} %copy-done, bf16[512,2,128,1]{0,2,3,1:T(8,128)(2,1)S(1)} %bitcast.73, f32[2,512,256,8]{2,1,3,0:T(8,128)S(1)} %get-tuple-element.654, f32[2,8,256]{2,1,0:T(8,128)S(1)} %max.9, pred[256,512]{0,1:T(8,128)(4,1)S(1)} %get-tuple-element.480, ...), kind=kOutput, calls=%fused_computation.25 | convolution fusion | flops 548405248 | bytes 13008896 | tf_op jit(solution)/shard_map/while/body/eval_jaxpr/cond/branch_1_fun/gjrl,lgd->gjrd/dot_general | solution.py:39
  156.4 1.3 copy-done.1
  159.2 9.4 %conditional.7 = ((f32[2,8,256]{2,1,0:T(8,128)S(1)}, f32[2,8,256]{2,1,0:T(8,128)S(1)}, f32[2,8,256,128]{3,2,1,0:T(8,128)})) conditional(s32[]{:T(128)} %convert_element_type.67, (f32[2,8,256]{2,1,0:T(8,128)S(1)}, f32[2,8,256]{2,1,0:T(8,128)S(1)}, f32[2,8,256,128]{3,2,1,0:T(8,128)}) %tuple.108, (pred[256,512]{0,1:T(8,128)(4,1)S(1)}, ...), branch_computations={%region_9.9_spmd, %region_10.12_spmd} | conditional | flops 1102061568 | bytes 49414236 | solution.py:50
  159.2 1.0 constant_dynamic-slice_fusion.2
  160.2 1.5 fusion.15
  161.8 2.0 fusion.17
  163.8 3.5 %multiply_add_fusion.2 = f32[2,8,256,128]{3,2,1,0:T(8,128)S(1)} fusion(f32[2,8,256,128]{3,2,1,0:T(8,128)S(1)} %copy-done, bf16[512,2,128,1]{0,2,3,1:T(8,128)(2,1)S(1)} %bitcast.73, f32[2,512,256,8]{2,1,3,0:T(8,128)S(1)} %get-tuple-element.654, f32[2,8,256]{2,1,0:T(8,128)S(1)} %max.9, pred[256,512]{0,1:T(8,128)(4,1)S(1)} %get-tuple-element.480, ...), kind=kOutput, calls=%fused_computation.25 | convolution fusion | flops 548405248 | bytes 13008896 | tf_op jit(solution)/shard_map/while/body/eval_jaxpr/cond/branch_1_fun/gjrl,lgd->gjrd/dot_general | solution.py:39
  167.3 1.3 copy-done.1
  170.1 9.4 %conditional.7 = ((f32[2,8,256]{2,1,0:T(8,128)S(1)}, f32[2,8,256]{2,1,0:T(8,128)S(1)}, f32[2,8,256,128]{3,2,1,0:T(8,128)})) conditional(s32[]{:T(128)} %convert_element_type.67, (f32[2,8,256]{2,1,0:T(8,128)S(1)}, f32[2,8,256]{2,1,0:T(8,128)S(1)}, f32[2,8,256,128]{3,2,1,0:T(8,128)}) %tuple.108, (pred[256,512]{0,1:T(8,128)(4,1)S(1)}, ...), branch_computations={%region_9.9_spmd, %region_10.12_spmd} | conditional | flops 1102061568 | bytes 49414236 | solution.py:50
  170.1 1.0 constant_dynamic-slice_fusion.2
  171.1 1.5 fusion.15
  172.7 2.0 fusion.17
  174.7 3.5 %multiply_add_fusion.2 = f32[2,8,256,128]{3,2,1,0:T(8,128)S(1)} fusion(f32[2,8,256,128]{3,2,1,0:T(8,128)S(1)} %copy-done, bf16[512,2,128,1]{0,2,3,1:T(8,128)(2,1)S(1)} %bitcast.73, f32[2,512,256,8]{2,1,3,0:T(8,128)S(1)} %get-tuple-element.654, f32[2,8,256]{2,1,0:T(8,128)S(1)} %max.9, pred[256,512]{0,1:T(8,128)(4,1)S(1)} %get-tuple-element.480, ...), kind=kOutput, calls=%fused_computation.25 | convolution fusion | flops 548405248 | bytes 13008896 | tf_op jit(solution)/shard_map/while/body/eval_jaxpr/cond/branch_1_fun/gjrl,lgd->gjrd/dot_general | solution.py:39
  178.2 1.3 copy-done.1
  181.0 9.4 %conditional.7 = ((f32[2,8,256]{2,1,0:T(8,128)S(1)}, f32[2,8,256]{2,1,0:T(8,128)S(1)}, f32[2,8,256,128]{3,2,1,0:T(8,128)})) conditional(s32[]{:T(128)} %convert_element_type.67, (f32[2,8,256]{2,1,0:T(8,128)S(1)}, f32[2,8,256]{2,1,0:T(8,128)S(1)}, f32[2,8,256,128]{3,2,1,0:T(8,128)}) %tuple.108, (pred[256,512]{0,1:T(8,128)(4,1)S(1)}, ...), branch_computations={%region_9.9_spmd, %region_10.12_spmd} | conditional | flops 1102061568 | bytes 49414236 | solution.py:50
  181.0 1.0 constant_dynamic-slice_fusion.2
  182.0 1.5 fusion.15
  183.6 2.0 fusion.17
  185.6 3.5 %multiply_add_fusion.2 = f32[2,8,256,128]{3,2,1,0:T(8,128)S(1)} fusion(f32[2,8,256,128]{3,2,1,0:T(8,128)S(1)} %copy-done, bf16[512,2,128,1]{0,2,3,1:T(8,128)(2,1)S(1)} %bitcast.73, f32[2,512,256,8]{2,1,3,0:T(8,128)S(1)} %get-tuple-element.654, f32[2,8,256]{2,1,0:T(8,128)S(1)} %max.9, pred[256,512]{0,1:T(8,128)(4,1)S(1)} %get-tuple-element.480, ...), kind=kOutput, calls=%fused_computation.25 | convolution fusion | flops 548405248 | bytes 13008896 | tf_op jit(solution)/shard_map/while/body/eval_jaxpr/cond/branch_1_fun/gjrl,lgd->gjrd/dot_general | solution.py:39
  189.1 1.3 copy-done.1
  190.4 1.9 fusion.27
  193.1 1.2 copy.57
  194.5 39.5 %while.36 = (s32[]{:T(128)}, f32[2,8,256]{2,1,0:T(8,128)S(1)}, f32[2,8,256]{2,1,0:T(8,128)S(1)}, f32[2,8,256,128]{3,2,1,0:T(8,128)S(1)}, s32[256]{0:T(256)S(1)},...) while((s32[]{:T(128)}, f32[2,8,256]{2,1,0:T(8,128)S(1)}, ...), condition=%wide.region_6.7_spmd.clone, body=%wide.region_0.6_spmd.clone.sunk | while | flops 1102586624 | bytes 32781632 | solution.py:70
  196.3 8.1 %conditional.6 = ((f32[2,8,256]{2,1,0:T(8,128)S(1)}, f32[2,8,256]{2,1,0:T(8,128)S(1)}, f32[2,8,256,128]{3,2,1,0:T(8,128)S(1)})) conditional(s32[]{:T(128)} %convert_element_type.66, (f32[2,8,256]{2,1,0:T(8,128)S(1)}, f32[2,8,256]{2,1,0:T(8,128)S(1)}, f32[2,8,256,128]{3,2,1,0:T(8,128)S(1)}) %tuple.104, (pred[256,512]{0,1:T(8,128)(4,1)S(1)}, ...), branch_computations={%region_2.2_spmd, %region_3.0_spmd} | conditional | flops 1102061568 | bytes 32636964 | solution.py:50
  196.3 1.1 constant_dynamic-slice_fusion
  197.4 1.5 fusion.4
  198.9 2.0 fusion.6
  200.9 3.5 %multiply_add_fusion = f32[2,8,256,128]{3,2,1,0:T(8,128)S(1)} fusion(f32[2,8,256,128]{3,2,1,0:T(8,128)S(1)} %get-tuple-element.463, bf16[512,2,128,1]{0,2,3,1:T(8,128)(2,1)S(1)} %bitcast.74, f32[2,512,256,8]{2,1,3,0:T(8,128)S(1)} %get-tuple-element.650, f32[2,8,256]{2,1,0:T(8,128)S(1)} %max.8, pred[256,512]{0,1:T(8,128)(4,1)S(1)} %get-tuple-element.458, ...), kind=kOutput, calls=%fused_computation.10 | convolution fusion | flops 548405248 | bytes 13008896 | tf_op jit(solution)/shard_map/while/body/eval_jaxpr/cond/branch_1_fun/gjrl,lgd->gjrd/dot_general | solution.py:39
  206.1 8.1 %conditional.6 = ((f32[2,8,256]{2,1,0:T(8,128)S(1)}, f32[2,8,256]{2,1,0:T(8,128)S(1)}, f32[2,8,256,128]{3,2,1,0:T(8,128)S(1)})) conditional(s32[]{:T(128)} %convert_element_type.66, (f32[2,8,256]{2,1,0:T(8,128)S(1)}, f32[2,8,256]{2,1,0:T(8,128)S(1)}, f32[2,8,256,128]{3,2,1,0:T(8,128)S(1)}) %tuple.104, (pred[256,512]{0,1:T(8,128)(4,1)S(1)}, ...), branch_computations={%region_2.2_spmd, %region_3.0_spmd} | conditional | flops 1102061568 | bytes 32636964 | solution.py:50
  206.2 1.1 constant_dynamic-slice_fusion
  207.2 1.5 fusion.4
  208.8 2.0 fusion.6
  210.8 3.5 %multiply_add_fusion = f32[2,8,256,128]{3,2,1,0:T(8,128)S(1)} fusion(f32[2,8,256,128]{3,2,1,0:T(8,128)S(1)} %get-tuple-element.463, bf16[512,2,128,1]{0,2,3,1:T(8,128)(2,1)S(1)} %bitcast.74, f32[2,512,256,8]{2,1,3,0:T(8,128)S(1)} %get-tuple-element.650, f32[2,8,256]{2,1,0:T(8,128)S(1)} %max.8, pred[256,512]{0,1:T(8,128)(4,1)S(1)} %get-tuple-element.458, ...), kind=kOutput, calls=%fused_computation.10 | convolution fusion | flops 548405248 | bytes 13008896 | tf_op jit(solution)/shard_map/while/body/eval_jaxpr/cond/branch_1_fun/gjrl,lgd->gjrd/dot_general | solution.py:39
  216.0 8.1 %conditional.6 = ((f32[2,8,256]{2,1,0:T(8,128)S(1)}, f32[2,8,256]{2,1,0:T(8,128)S(1)}, f32[2,8,256,128]{3,2,1,0:T(8,128)S(1)})) conditional(s32[]{:T(128)} %convert_element_type.66, (f32[2,8,256]{2,1,0:T(8,128)S(1)}, f32[2,8,256]{2,1,0:T(8,128)S(1)}, f32[2,8,256,128]{3,2,1,0:T(8,128)S(1)}) %tuple.104, (pred[256,512]{0,1:T(8,128)(4,1)S(1)}, ...), branch_computations={%region_2.2_spmd, %region_3.0_spmd} | conditional | flops 1102061568 | bytes 32636964 | solution.py:50
  216.0 1.1 constant_dynamic-slice_fusion
  217.1 1.5 fusion.4
  218.6 2.0 fusion.6
  220.7 3.5 %multiply_add_fusion = f32[2,8,256,128]{3,2,1,0:T(8,128)S(1)} fusion(f32[2,8,256,128]{3,2,1,0:T(8,128)S(1)} %get-tuple-element.463, bf16[512,2,128,1]{0,2,3,1:T(8,128)(2,1)S(1)} %bitcast.74, f32[2,512,256,8]{2,1,3,0:T(8,128)S(1)} %get-tuple-element.650, f32[2,8,256]{2,1,0:T(8,128)S(1)} %max.8, pred[256,512]{0,1:T(8,128)(4,1)S(1)} %get-tuple-element.458, ...), kind=kOutput, calls=%fused_computation.10 | convolution fusion | flops 548405248 | bytes 13008896 | tf_op jit(solution)/shard_map/while/body/eval_jaxpr/cond/branch_1_fun/gjrl,lgd->gjrd/dot_general | solution.py:39
  225.9 8.1 %conditional.6 = ((f32[2,8,256]{2,1,0:T(8,128)S(1)}, f32[2,8,256]{2,1,0:T(8,128)S(1)}, f32[2,8,256,128]{3,2,1,0:T(8,128)S(1)})) conditional(s32[]{:T(128)} %convert_element_type.66, (f32[2,8,256]{2,1,0:T(8,128)S(1)}, f32[2,8,256]{2,1,0:T(8,128)S(1)}, f32[2,8,256,128]{3,2,1,0:T(8,128)S(1)}) %tuple.104, (pred[256,512]{0,1:T(8,128)(4,1)S(1)}, ...), branch_computations={%region_2.2_spmd, %region_3.0_spmd} | conditional | flops 1102061568 | bytes 32636964 | solution.py:50
  225.9 1.1 constant_dynamic-slice_fusion
  227.0 1.5 fusion.4
  228.5 2.0 fusion.6
  230.5 3.5 %multiply_add_fusion = f32[2,8,256,128]{3,2,1,0:T(8,128)S(1)} fusion(f32[2,8,256,128]{3,2,1,0:T(8,128)S(1)} %get-tuple-element.463, bf16[512,2,128,1]{0,2,3,1:T(8,128)(2,1)S(1)} %bitcast.74, f32[2,512,256,8]{2,1,3,0:T(8,128)S(1)} %get-tuple-element.650, f32[2,8,256]{2,1,0:T(8,128)S(1)} %max.8, pred[256,512]{0,1:T(8,128)(4,1)S(1)} %get-tuple-element.458, ...), kind=kOutput, calls=%fused_computation.10 | convolution fusion | flops 548405248 | bytes 13008896 | tf_op jit(solution)/shard_map/while/body/eval_jaxpr/cond/branch_1_fun/gjrl,lgd->gjrd/dot_general | solution.py:39
  235.7 3.7 %maximum_select_fusion = bf16[256,4096]{1,0:T(8,128)(2,1)} fusion(bf16[256,2048]{1,0:T(8,128)(2,1)} %collective-permute-done.4, bf16[256,2048]{1,0:T(8,128)(2,1)S(1)} %bitcast.75, pred[]{:T(512)S(6)} %eq.69), kind=kLoop, calls=%fused_computation.39 | loop fusion | flops 9437184 | bytes 4194305 | tf_op jit(solution)/shard_map/jit(_where)/select_n | solution.py:149
  (95 shorter events, 12.4 us)
Async XLA Ops:
  6.5 57.1 %all-gather.4.cloned.1.call-start = ((), (), s32[]{:S(2)}) async-start(), calls=%async_computation | async-start | bytes 2359296 | tf_op jit(solution)/shard_map/all_gather | solution.py:112
  8.4 111.1 %all-gather.6.cloned.1.call-start = ((), (), s32[]{:S(2)}) async-start(), calls=%async_computation.1 | async-start | bytes 2359296 | tf_op jit(solution)/shard_map/all_gather | solution.py:113
  13.3 130.3 %collective-permute-start.2 = (bf16[256,2048]{0,1:T(8,128)(2,1)}, bf16[256,2048]{0,1:T(8,128)(2,1)}, u32[]{:S(2)}, u32[]{:S(2)}) collective-permute-start(bf16[256,2048]{0,1:T(8,128)(2,1)} %copy.52), channel_id=1, source_target_pairs={{0,8},{8,0},{16,24},{24,16},{32,40},{40,32},{48,56},{56,48},{64,72... | collective-permute-start | bytes 3145736 | tf_op jit(solution)/shard_map/ppermute | solution.py:19
  13.9 111.7 %copy-start.2 = (s32[256]{0:T(256)S(1)}, s32[256]{0:T(256)}, u32[]{:S(2)}) copy-start(s32[256]{0:T(256)} %param.15) | copy-start | bytes 3076
  66.7 78.5 %collective-permute-start.1 = (bf16[2048,256]{0,1:T(8,128)(2,1)}, bf16[2048,256]{0,1:T(8,128)(2,1)S(1)}, u32[]{:S(2)}, u32[]{:S(2)}) collective-permute-start(bf16[2048,256]{0,1:T(8,128)(2,1)} %get-tuple-element.662), channel_id=1, source_target_pairs={{0,8},{8,0},{16,24},{24,16},{32,40},{40,32},{48,56},{56,48},{64,72... | collective-permute-start | bytes 3145736 | tf_op jit(solution)/shard_map/ppermute | solution.py:19
  122.7 22.6 %collective-permute-start.3 = (bf16[2048,256]{0,1:T(8,128)(2,1)}, bf16[2048,256]{0,1:T(8,128)(2,1)}, u32[]{:S(2)}, u32[]{:S(2)}) collective-permute-start(bf16[2048,256]{0,1:T(8,128)(2,1)} %get-tuple-element.658), channel_id=1, source_target_pairs={{0,8},{8,0},{16,24},{24,16},{32,40},{40,32},{48,56},{56,48},{64,72... | collective-permute-start | bytes 3145736 | tf_op jit(solution)/shard_map/ppermute | solution.py:19
  137.2 4.7 %collective-permute-start = (s32[2048]{0:T(1024)S(1)}, s32[2048]{0:T(1024)S(1)}, u32[]{:S(2)}, u32[]{:S(2)}) collective-permute-start(s32[2048]{0:T(1024)S(1)} %bitcast.79), channel_id=1, source_target_pairs={{0,8},{8,0},{16,24},{24,16},{32,40},{40,32},{48,56},{56,48},{64,72... | collective-permute-start | bytes 24584 | tf_op jit(solution)/shard_map/ppermute | solution.py:19
  150.9 2.0 copy-start
  156.4 1.3 copy-start.1
  161.8 2.0 copy-start
  167.3 1.3 copy-start.1
  172.7 2.0 copy-start
  178.2 1.3 copy-start.1
  183.6 2.0 copy-start
  189.1 1.3 copy-start.1
  194.3 41.4 %collective-permute-start.4 = (bf16[256,2048]{1,0:T(8,128)(2,1)}, bf16[256,2048]{1,0:T(8,128)(2,1)}, u32[]{:S(2)}, u32[]{:S(2)}) collective-permute-start(bf16[256,2048]{1,0:T(8,128)(2,1)} %bitcast.69), channel_id=1, source_target_pairs={{0,8},{8,0},{16,24},{24,16},{32,40},{40,32},{48,56},{56,48},{64,72... | collective-permute-start | bytes 3145736 | tf_op jit(solution)/shard_map/ppermute | solution.py:19
Sparse Core Ops, SparseCore 0:
  9.1 54.4 all-gather.3
  65.3 54.1 all-gather.5
where the time goes:
time: 247 us; the launch traced here: 246 us
  waiting for transfers between devices  99.5 us (40%)
  matrix products  39.9 us (16%)
  local copies, waits for them, and re-layouts  36.3 us (15%)
  other arithmetic  29.6 us (12%)
  between operations  13.6 us (6%)
  blocking collectives  11.5 us (5%)
  starting transfers between devices  10.1 us (4%)
  loops' own time  5.78 us (2%)
    all_gather x1, waiting for transfers between devices, local(): lax.all_gather(values, 'ctx', axis=0, tiled=True)  49.8 us
    all_gather x1, waiting for transfers between devices, local(): lax.all_gather(keys, 'ctx', axis=0, tiled=True)  49.6 us
    dot_general x8, matrix products, compute(): jnp.einsum('gjrl,lgd->gjrd', weights.astype(jnp.bfloat16), heads_v, prefe...  27.7 us
    reduce_sum x8, other arithmetic, compute(): totals = totals * rescale + jnp.sum(weights, axis=-1)  16 us
    dot_general x8, matrix products, compute(): jnp.einsum('rgjd,lgd->gjrl', heads_q, heads_k, preferred_element_type=jnp...  12.2 us
    all_gather x1, blocking collectives, local(): lax.all_gather(segments, 'ctx', axis=0, tiled=True)  11.5 us
    ppermute x5, starting transfers between devices, swapped(): return lax.ppermute(value, axis, pairs)  10.1 us
    unnamed x10, local copies, waits for them, and re-layouts  9.21 us
  transfers between devices with their start and end apart: 7, of which 2 were waited for; matrix products, arithmetic and copies ran while one was open for 22% of the time, Pallas kernels for 0%

commit v1 on v0

v1 whole, which is shorter than its diff:
```python
import functools
import math

import jax
import jax.numpy as jnp
from jax import lax
from jax.experimental import pallas as pl
from jax.experimental.pallas import tpu as pltpu
from jax.sharding import PartitionSpec as P

QH = 32
KVH = 4
HD = 128
TOK = 256
SUB = 128
TAG = 16
PER = QH // KVH
SCALE = math.log2(math.e) / math.sqrt(HD)
SHUT = -1e30
OPEN = 3e38
SAFE = 1e30


def caps_of(tag_q, tag_k, earlier):
    key_docs = tag_k[...].astype(jnp.float32)
    key_docs = jnp.where(earlier, key_docs, -1.0)
    row = jnp.concatenate([key_docs[0:1], key_docs[8:9]], axis=1)
    query_docs = tag_q[...].astype(jnp.float32)
    caps = []
    for half in range(2):
        own = query_docs[8 * half : 8 * half + 1]
        own = jnp.concatenate([own, own], axis=1)
        caps.append(jnp.broadcast_to(jnp.where(row == own, OPEN, SHUT), (SUB, TOK)))
    return jnp.concatenate(caps, axis=0)


def own_cap(tag):
    docs = tag[...].astype(jnp.float32)
    rows = lax.broadcasted_iota(jnp.int32, (TOK, TOK), 0)
    cols = lax.broadcasted_iota(jnp.int32, (TOK, TOK), 1)
    same = jnp.broadcast_to(jnp.where(docs[0:1] == docs[8:9], 1, 0), (SUB, SUB))
    ones = jnp.ones((SUB, SUB), jnp.int32)
    same = jnp.concatenate(
        [
            jnp.concatenate([ones, ones], axis=1),
            jnp.concatenate([same, ones], axis=1),
        ],
        axis=0,
    )
    return jnp.where((cols <= rows) & (same == 1), OPEN, SHUT)


def scores_of(rows, keys):
    return lax.dot_general(
        rows, keys, (((1,), (1,)), ((), ())), preferred_element_type=jnp.float32
    )


def attend_kernel(blocks, own, first, last, others, *refs):
    refs = iter(refs)
    flags, query, own_keys, own_values = (next(refs) for _ in range(4))
    keys = [next(refs) for _ in range(blocks)]
    values = [next(refs) for _ in range(blocks)]
    if not first:
        mixed_in, totals_in = next(refs), next(refs)
    if last:
        far_keys = [next(refs) for _ in range(others)]
        far_values = [next(refs) for _ in range(others)]
        out = next(refs)
        key_buf, value_buf, sem = next(refs), next(refs), next(refs)
    else:
        mixed_out, totals_out = next(refs), next(refs)
    tag = own_values.at[TOK : TOK + TAG]
    self_keys = own_keys[...].astype(jnp.float32)

    parts = []
    if own:
        parts.append((own_keys[...], own_values[:TOK], own_cap(tag)))
    for at in range(blocks):
        cap = caps_of(tag, values[at].at[TOK : TOK + TAG], flags[at] > 0)
        parts.append((keys[at][...], values[at][:TOK], cap))

    lane = lax.broadcasted_iota(jnp.int32, (TOK, HD), 1)
    totals = None if first else totals_in[0]
    worst = None
    for head in range(PER):
        span = slice(head * HD, (head + 1) * HD)
        rows = query[:, span]
        shift = SCALE * jnp.sum(rows.astype(jnp.float32) * self_keys, axis=1, keepdims=True)
        mixed = None
        mark = jnp.where(lane == head, 1.0, 0.0).astype(jnp.bfloat16)
        if last:
            mark = jnp.ones((TOK, HD), jnp.bfloat16)
        for block_keys, block_values, cap in parts:
            scores = scores_of(rows, block_keys)
            weights = jnp.exp2(jnp.minimum(scores * SCALE - shift, cap)).astype(jnp.bfloat16)
            added = jnp.dot(
                weights,
                jnp.concatenate([block_values, mark], axis=1),
                preferred_element_type=jnp.float32,
            )
            mixed = added if mixed is None else mixed + added
        sums = mixed[:, HD:]
        mixed = mixed[:, :HD]
        if not first:
            mixed = mixed + mixed_in[:, span]
        if last:
            sums = sums + jnp.broadcast_to(totals[:, head : head + 1], (TOK, HD))
            out[:, span] = (mixed / sums).astype(jnp.bfloat16)
            high = jnp.where(sums < SAFE, 0.0, 1.0)
            worst = high if worst is None else jnp.maximum(worst, high)
        else:
            mixed_out[:, span] = mixed
            totals = sums if totals is None else totals + sums
    if not last:
        totals_out[0] = totals
        return

    group = pl.program_id(0)

    @pl.when(jnp.max(worst) > 0.0)
    def _():
        cols = pl.ds(pl.multiple_of(group * HD, HD), HD)
        for at in range(others):
            for source, target in ((far_keys, key_buf), (far_values, value_buf)):
                copy = pltpu.make_async_copy(source[at].at[:, cols], target.at[at], sem)
                copy.start()
                copy.wait()
        local = [(own_keys, own_values, None)]
        local += [(keys[at], values[at], flags[at]) for at in range(blocks)]
        local += [
            (key_buf.at[at], value_buf.at[at], flags[blocks + at]) for at in range(others)
        ]

        def capped(rows, place):
            block_keys, block_values, flag = local[place]
            scores = scores_of(rows, block_keys[...]) * SCALE
            if flag is None:
                return jnp.minimum(scores, own_cap(tag))
            return jnp.minimum(scores, caps_of(tag, block_values.at[TOK : TOK + TAG], flag > 0))

        def one_head(head, carry):
            span = pl.ds(pl.multiple_of(head * HD, HD), HD)
            rows = query[:, span]
            top = None
            for place in range(len(local)):
                high = jnp.max(capped(rows, place), axis=1, keepdims=True)
                top = high if top is None else jnp.maximum(top, high)
            mixed = jnp.zeros((TOK, 2 * HD), jnp.float32)
            for place in range(len(local)):
                weights = jnp.exp2(capped(rows, place) - top).astype(jnp.bfloat16)
                block_values = local[place][1][:TOK]
                mixed = mixed + jnp.dot(
                    weights,
                    jnp.concatenate([block_values, jnp.ones_like(block_values)], axis=1),
                    preferred_element_type=jnp.float32,
                )
            out[:, span] = (mixed[:, :HD] / mixed[:, HD:]).astype(jnp.bfloat16)
            return carry

        lax.fori_loop(0, PER, one_head, 0)


def attend(name, flags, query, own_pair, pairs, state=None, own=False, far=None, base=0, groups=KVH):
    blocks = len(pairs)
    first, last = state is None, far is not None
    wide = pl.BlockSpec((TOK, PER * HD), lambda g: (0, g + base))
    key_spec = pl.BlockSpec((TOK, HD), lambda g: (0, g + base))
    value_spec = pl.BlockSpec((TOK + TAG, HD), lambda g: (0, g + base))
    mixed_spec = pl.BlockSpec((TOK, PER * HD), lambda g: (0, g))
    total_spec = pl.BlockSpec((1, TOK, HD), lambda g: (g, 0, 0))
    anywhere = pl.BlockSpec(memory_space=pl.ANY)
    args = [flags, query, *own_pair, *(k for k, _ in pairs), *(v for _, v in pairs)]
    in_specs = [pl.BlockSpec(memory_space=pltpu.SMEM), wide, key_spec, value_spec]
    in_specs += [key_spec] * blocks + [value_spec] * blocks
    if not first:
        args += list(state)
        in_specs += [mixed_spec, total_spec]
    scratch = []
    if last:
        args += [k for k, _ in far] + [v for _, v in far]
        in_specs += [anywhere] * (2 * len(far))
        out_shape = jax.ShapeDtypeStruct((TOK, QH * HD), jnp.bfloat16)
        out_specs = wide
        scratch = [
            pltpu.VMEM((len(far), TOK, HD), jnp.bfloat16),
            pltpu.VMEM((len(far), TOK + TAG, HD), jnp.bfloat16),
            pltpu.SemaphoreType.DMA,
        ]
    else:
        out_shape = (
            jax.ShapeDtypeStruct((TOK, groups * PER * HD), jnp.float32),
            jax.ShapeDtypeStruct((groups, TOK, HD), jnp.float32),
        )
        out_specs = (mixed_spec, total_spec)
    work = (blocks + (1 if own else 0)) * groups * PER * TOK * TOK
    return pl.pallas_call(
        functools.partial(attend_kernel, blocks, own, first, last, len(far) if last else 0),
        grid=(groups,),
        in_specs=in_specs,
        out_specs=out_specs,
        out_shape=out_shape,
        scratch_shapes=scratch,
        compiler_params=pltpu.CompilerParams(vmem_limit_bytes=32 * 2**20),
        cost_estimate=pl.CostEstimate(
            flops=work * HD * 4, bytes_accessed=6 * 2**20, transcendentals=work
        ),
        name=name,
    )(*args)


def move(value, step_y, step_z):
    pairs = []
    for source in range(8):
        y, z = source // 2, source % 2
        pairs.append((source, (y + step_y) % 4 * 2 + (z + step_z) % 2))
    return lax.ppermute(value, "ctx", pairs)


def local(query, keys, values, segments):
    place = lax.axis_index("ctx")
    y, z = place // 2, place % 2

    up = functools.partial(move, step_y=1, step_z=0)
    down = functools.partial(move, step_y=-1, step_z=0)
    over = functools.partial(move, step_y=0, step_z=1)

    docs = segments.astype(jnp.bfloat16)
    tag = jnp.concatenate(
        [jnp.broadcast_to(docs[at * SUB], (TAG // 2, KVH * HD)) for at in range(2)], axis=0
    )
    tagged = jnp.concatenate([values, tag], axis=0)

    k_up, k_down, k_over = up(keys), down(keys), over(keys)
    v_up, v_down, v_over = up(tagged), down(tagged), over(tagged)
    k_far, v_far = up(k_up), down(v_down)
    k_up_over, k_down_over = over(k_up), over(k_down)
    v_up_over, v_down_over = up(v_over), down(v_over)
    k_far_over, v_far_over = up(k_up_over), down(v_down_over)

    own = (keys, tagged)
    near = [(k_up, v_up), (k_down, v_down), (k_over, v_over)]
    mid = [(k_far, v_far), (k_up_over, v_up_over), (k_down_over, v_down_over)]
    end = [(k_far_over, v_far_over)]

    def flags_of(steps):
        return jnp.stack(
            [((y + dy) % 4 * 2 + (z + dz) % 2 < place).astype(jnp.int32) for dy, dz in steps]
        )

    near_steps = [(-1, 0), (1, 0), (0, 1)]
    mid_steps = [(2, 0), (-1, 1), (1, 1)]
    end_steps = [(2, 1)]
    state = attend("near", flags_of(near_steps), query, own, near, own=True)
    state = attend("mid", flags_of(mid_steps), query, own, mid, state)
    return attend(
        "end", flags_of(end_steps + near_steps + mid_steps), query, own, end, state, far=near + mid
    )


def solution(mesh):
    placed = (
        P(("dp", "ctx"), None),
        P(("dp", "ctx"), None),
        P(("dp", "ctx"), None),
        P(("dp", "ctx")),
    )
    return jax.shard_map(
        local, mesh=mesh, in_specs=placed, out_specs=P(("dp", "ctx"), None), check_vma=False
    )
```

time: 247 us -> 65 us (0.26)
  the two profiles are of different devices: /device:TPU:31 before, /device:TPU:4 now
where the time goes in v1:
time: 65 us; the launch traced here: 64.8 us
  Pallas kernels  27.9 us (43%)
  starting transfers between devices  20.7 us (32%)
  waiting for transfers between devices  9.47 us (15%)
  local copies, waits for them, and re-layouts  4.44 us (7%)
  other arithmetic  1.92 us (3%)
    pallas_call x3, Pallas kernels, attend(): pl.pallas_call(functools.partial(attend_kernel, blocks, own, first, last,...  27.9 us
    ppermute x14, starting transfers between devices, move(): return lax.ppermute(value, 'ctx', pairs)  20.7 us
    ppermute x14, waiting for transfers between devices, move(): return lax.ppermute(value, 'ctx', pairs)  9.47 us
    unnamed x8, local copies, waits for them, and re-layouts  2.55 us
  transfers between devices with their start and end apart: 14, of which 2 were waited for; matrix products, arithmetic and copies ran while one was open for 6% of the time, Pallas kernels for 32%

profile of v1, /device:TPU:4, one launch (start us, length us, event | category | flops | bytes accessed | tf_op | source)
XLA Modules:
  0.0 64.8 jit_solution(15168719859636642332)
XLA Ops:
  0.0 1.6 %collective-permute-start = (bf16[256,512]{1,0:T(8,128)(2,1)}, bf16[256,512]{1,0:T(8,128)(2,1)S(1)}, u32[]{:S(2)}, u32[]{:S(2)}) collective-permute-start(bf16[256,512]{1,0:T(8,128)(2,1)} %refs_2_.5), channel_id=1, source_target_pairs={{0,2},{1,3},{2,4},{3,5},{4,6},{5,7},{6,0},{7,1},{8,10},{9,11},{10,... | collective-permute-start | bytes 786440 | tf_op jit(solution)/shard_map/ppermute | solution.py:217
  1.6 1.7 %collective-permute-start.7 = (bf16[256,512]{1,0:T(8,128)(2,1)}, bf16[256,512]{1,0:T(8,128)(2,1)S(1)}, u32[]{:S(2)}, u32[]{:S(2)}) collective-permute-start(bf16[256,512]{1,0:T(8,128)(2,1)} %refs_2_.5), channel_id=1, source_target_pairs={{0,6},{1,7},{2,0},{3,1},{4,2},{5,3},{6,4},{7,5},{8,14},{9,15},{10,... | collective-permute-start | bytes 786440 | tf_op jit(solution)/shard_map/ppermute | solution.py:217
  3.2 0.7 %convert_element_type.2 = bf16[256]{0:T(256)(128)(2,1)S(1)} convert(s32[256]{0:T(256)} %param.7) | non-fusion elementwise | flops 256 | bytes 1536 | tf_op jit(solution)/shard_map/convert_element_type | solution.py:228
  3.9 0.5 fusion
  4.4 0.6 broadcast_in_dim.6
  5.1 0.6 broadcast_in_dim.7
  5.7 0.1 pad.8.clone
  5.8 1.1 %maximum_maximum_fusion.refs_3_ = bf16[272,512]{1,0:T(8,128)(2,1)S(1)} fusion(bf16[256,512]{1,0:T(8,128)(2,1)} %param.6, bf16[272]{0:T(512)(128)(2,1)S(1)} %pad.8.clone, bf16[272]{0:T(512)(128)(2,1)S(1)} %pad.7.clone), kind=kLoop, calls=%fused_computation | loop fusion | flops 835584 | bytes 541760 | tf_op jit(solution)/shard_map/concatenate | solution.py:232
  6.8 2.0 %collective-permute-start.3 = (bf16[272,512]{1,0:T(8,128)(2,1)S(1)}, bf16[272,512]{1,0:T(8,128)(2,1)S(1)}, u32[]{:S(2)}, u32[]{:S(2)}) collective-permute-start(bf16[272,512]{1,0:T(8,128)(2,1)S(1)} %maximum_maximum_fusion.refs_3_), channel_id=1, source_target_pairs={{0,1},{1,0},{2,3},{3,2},{4,5},{5,4},{6,7},{7,6},{8,9},{9,8},{10,11... | collective-permute-start | bytes 835592 | tf_op jit(solution)/shard_map/ppermute | solution.py:217
  8.9 1.8 %collective-permute-start.9 = (bf16[272,512]{1,0:T(8,128)(2,1)S(1)}, bf16[272,512]{1,0:T(8,128)(2,1)S(1)}, u32[]{:S(2)}, u32[]{:S(2)}) collective-permute-start(bf16[272,512]{1,0:T(8,128)(2,1)S(1)} %maximum_maximum_fusion.refs_3_), channel_id=1, source_target_pairs={{0,6},{1,7},{2,0},{3,1},{4,2},{5,3},{6,4},{7,5},{8,14},{9,15},{10,... | collective-permute-start | bytes 835592 | tf_op jit(solution)/shard_map/ppermute | solution.py:217
  10.7 0.2 collective-permute-start.13
  10.9 0.0 collective-permute-done.refs_4_.refs_8_
  10.9 0.6 collective-permute-start.12
  11.4 0.0 collective-permute-done.7.refs_5_.refs_9_
  11.4 1.5 %collective-permute-start.1 = (bf16[256,512]{1,0:T(8,128)(2,1)S(1)}, bf16[256,512]{1,0:T(8,128)(2,1)S(1)}, u32[]{:S(2)}, u32[]{:S(2)}) collective-permute-start(bf16[256,512]{1,0:T(8,128)(2,1)S(1)} %collective-permute-done.refs_4_.refs_8_), channel_id=1, source_target_pairs={{0,1},{1,0},{2,3},{3,2},{4,5},{5,4},{6,7},{7,6},{8,9},{9,8},{10,11... | collective-permute-start | bytes 786440 | tf_op jit(solution)/shard_map/ppermute | solution.py:217
  12.9 0.1 stack.71.refs_0_
  13.0 0.1 pad_add_fusion.1.refs_0_
  13.1 0.1 pad_add_fusion.refs_0_
  13.2 9.0 %collective-permute-done.12.refs_6_.refs_10_ = bf16[256,512]{1,0:T(8,128)(2,1)S(1)} collective-permute-done((bf16[256,512]{1,0:T(8,128)(2,1)}, bf16[256,512]{1,0:T(8,128)(2,1)S(1)}, u32[]{:S(2)}, u32[]{:S(2)}) %collective-permute-start.12) | collective-permute-done | bytes 262176 | tf_op jit(solution)/shard_map/ppermute | solution.py:217
  22.1 0.4 collective-permute-start.6
  22.5 0.0 collective-permute-done.3.refs_9_.refs_16_
  22.5 1.9 %collective-permute-start.8 = (bf16[256,512]{1,0:T(8,128)(2,1)S(1)}, bf16[256,512]{1,0:T(8,128)(2,1)S(1)}, u32[]{:S(2)}, u32[]{:S(2)}) collective-permute-start(bf16[256,512]{1,0:T(8,128)(2,1)S(1)} %collective-permute-done.7.refs_5_.refs_9_), channel_id=1, source_target_pairs={{0,1},{1,0},{2,3},{3,2},{4,5},{5,4},{6,7},{7,6},{8,9},{9,8},{10,11... | collective-permute-start | bytes 786440 | tf_op jit(solution)/shard_map/ppermute | solution.py:217
  24.4 0.0 collective-permute-done.9.refs_8_.refs_15_
  24.4 2.9 %collective-permute-start.4 = (bf16[272,512]{1,0:T(8,128)(2,1)S(1)}, bf16[272,512]{1,0:T(8,128)(2,1)S(1)}, u32[]{:S(2)}, u32[]{:S(2)}) collective-permute-start(bf16[272,512]{1,0:T(8,128)(2,1)S(1)} %collective-permute-done.3.refs_9_.refs_16_), channel_id=1, source_target_pairs={{0,6},{1,7},{2,0},{3,1},{4,2},{5,3},{6,4},{7,5},{8,14},{9,15},{10,... | collective-permute-start | bytes 835592 | tf_op jit(solution)/shard_map/ppermute | solution.py:217
  27.3 0.0 collective-permute-done.13.refs_7_.refs_14_
  27.3 0.0 collective-permute-start.11
  27.3 0.4 collective-permute-done.1.refs_5_.refs_12_
  27.8 2.8 %collective-permute-start.10 = (bf16[272,512]{1,0:T(8,128)(2,1)S(1)}, bf16[272,512]{1,0:T(8,128)(2,1)S(1)}, u32[]{:S(2)}, u32[]{:S(2)}) collective-permute-start(bf16[272,512]{1,0:T(8,128)(2,1)S(1)} %collective-permute-done.9.refs_8_.refs_15_), channel_id=1, source_target_pairs={{0,6},{1,7},{2,0},{3,1},{4,2},{5,3},{6,4},{7,5},{8,14},{9,15},{10,... | collective-permute-start | bytes 835592 | tf_op jit(solution)/shard_map/ppermute | solution.py:217
  30.6 0.0 copy-start
  30.6 1.6 %copy-done = bf16[256,4096]{1,0:T(8,128)(2,1)S(1)} copy-done((bf16[256,4096]{1,0:T(8,128)(2,1)S(1)}, bf16[256,4096]{1,0:T(8,128)(2,1)}, u32[]{:S(2)}) %copy-start) | copy-done | bytes 2097176
  32.1 0.0 copy-start.2
  32.1 0.9 %copy-done.2 = bf16[256,512]{1,0:T(8,128)(2,1)S(1)} copy-done((bf16[256,512]{1,0:T(8,128)(2,1)S(1)}, bf16[256,512]{1,0:T(8,128)(2,1)}, u32[]{:S(2)}) %copy-start.2) | copy-done | bytes 262168
  33.1 0.0 copy-start.1
  33.1 0.0 copy-start.3
  33.1 11.5 %near.1 = (f32[256,4096]{1,0:T(8,128)S(1)}, f32[4,256,128]{2,1,0:T(8,128)S(1)}) custom-call(s32[3]{0:T(128)S(1)} %pad_add_fusion.1.refs_0_, bf16[256,4096]{1,0:T(8,128)(2,1)S(1)} %copy-done, bf16[256,512]{1,0:T(8,128)(2,1)S(1)} %copy-done.2, bf16[272,512]{1,0:T(8,128)(2,1)S(1)} %maximum_maximum_fusion.refs_3_, ...), custom_call_target="tpu_custom_call" | custom-call | flops 4294967296 | bytes 6291456 | tf_op jit(solution)/shard_map/near/pallas_call | solution.py:197
  44.6 0.0 collective-permute-done.6.refs_4_.refs_11_
  44.6 0.3 collective-permute-start.2
  44.9 0.0 collective-permute-done.4.refs_9_.refs_19_
  44.9 3.2 %collective-permute-start.5 = (bf16[272,512]{1,0:T(8,128)(2,1)S(1)}, bf16[272,512]{1,0:T(8,128)(2,1)S(1)}, u32[]{:S(2)}, u32[]{:S(2)}) collective-permute-start(bf16[272,512]{1,0:T(8,128)(2,1)S(1)} %collective-permute-done.4.refs_9_.refs_19_), channel_id=1, source_target_pairs={{0,6},{1,7},{2,0},{3,1},{4,2},{5,3},{6,4},{7,5},{8,14},{9,15},{10,... | collective-permute-start | bytes 835592 | tf_op jit(solution)/shard_map/ppermute | solution.py:217
  48.1 0.0 collective-permute-done.8.refs_6_.refs_13_
  48.1 0.0 collective-permute-done.11.refs_8_.refs_18_
  48.1 0.0 collective-permute-done.10.refs_7_.refs_17_
  48.1 0.0 copy-done.1
  48.1 0.0 copy-done.3
  48.1 9.6 %mid.1 = (f32[256,4096]{1,0:T(8,128)S(1)}, f32[4,256,128]{2,1,0:T(8,128)S(1)}) custom-call(s32[3]{0:T(128)S(1)} %pad_add_fusion.refs_0_, bf16[256,4096]{1,0:T(8,128)(2,1)S(1)} %copy-done.1, bf16[256,512]{1,0:T(8,128)(2,1)S(1)} %copy-done.3, bf16[272,512]{1,0:T(8,128)(2,1)S(1)} %maximum_maximum_fusion.refs_3_, ...), custom_call_target="tpu_custom_call" | custom-call | flops 3221225472 | bytes 6291456 | tf_op jit(solution)/shard_map/mid/pallas_call | solution.py:197
  57.7 0.0 collective-permute-done.2.refs_4_
  57.7 0.0 collective-permute-done.5.refs_5_
  57.7 6.9 %end.1 = bf16[256,4096]{1,0:T(8,128)(2,1)} custom-call(s32[7]{0:T(128)S(1)} %stack.71.refs_0_, bf16[256,4096]{1,0:T(8,128)(2,1)S(1)} %copy-done.1, bf16[256,512]{1,0:T(8,128)(2,1)S(1)} %copy-done.3, bf16[272,512]{1,0:T(8,128)(2,1)S(1)} %maximum_maximum_fusion.refs_3_, bf16[256,512]{1,0:T(8,128)(2,1)S(1)} %collective-permute-done.2.refs_4_, ...), custom_call_target="tpu_custom_call" | custom-call | flops 1073741824 | bytes 6291456 | tf_op jit(solution)/shard_map/end/pallas_call | solution.py:197
  (1 shorter events, 0.0 us)
Async XLA Ops:
  0.0 10.9 %collective-permute-start = (bf16[256,512]{1,0:T(8,128)(2,1)}, bf16[256,512]{1,0:T(8,128)(2,1)S(1)}, u32[]{:S(2)}, u32[]{:S(2)}) collective-permute-start(bf16[256,512]{1,0:T(8,128)(2,1)} %refs_2_.5), channel_id=1, source_target_pairs={{0,2},{1,3},{2,4},{3,5},{4,6},{5,7},{6,0},{7,1},{8,10},{9,11},{10,... | collective-permute-start | bytes 786440 | tf_op jit(solution)/shard_map/ppermute | solution.py:217
  1.6 9.9 %collective-permute-start.7 = (bf16[256,512]{1,0:T(8,128)(2,1)}, bf16[256,512]{1,0:T(8,128)(2,1)S(1)}, u32[]{:S(2)}, u32[]{:S(2)}) collective-permute-start(bf16[256,512]{1,0:T(8,128)(2,1)} %refs_2_.5), channel_id=1, source_target_pairs={{0,6},{1,7},{2,0},{3,1},{4,2},{5,3},{6,4},{7,5},{8,14},{9,15},{10,... | collective-permute-start | bytes 786440 | tf_op jit(solution)/shard_map/ppermute | solution.py:217
  6.8 15.7 %collective-permute-start.3 = (bf16[272,512]{1,0:T(8,128)(2,1)S(1)}, bf16[272,512]{1,0:T(8,128)(2,1)S(1)}, u32[]{:S(2)}, u32[]{:S(2)}) collective-permute-start(bf16[272,512]{1,0:T(8,128)(2,1)S(1)} %maximum_maximum_fusion.refs_3_), channel_id=1, source_target_pairs={{0,1},{1,0},{2,3},{3,2},{4,5},{5,4},{6,7},{7,6},{8,9},{9,8},{10,11... | collective-permute-start | bytes 835592 | tf_op jit(solution)/shard_map/ppermute | solution.py:217
  8.9 15.6 %collective-permute-start.9 = (bf16[272,512]{1,0:T(8,128)(2,1)S(1)}, bf16[272,512]{1,0:T(8,128)(2,1)S(1)}, u32[]{:S(2)}, u32[]{:S(2)}) collective-permute-start(bf16[272,512]{1,0:T(8,128)(2,1)S(1)} %maximum_maximum_fusion.refs_3_), channel_id=1, source_target_pairs={{0,6},{1,7},{2,0},{3,1},{4,2},{5,3},{6,4},{7,5},{8,14},{9,15},{10,... | collective-permute-start | bytes 835592 | tf_op jit(solution)/shard_map/ppermute | solution.py:217
  10.7 16.7 %collective-permute-start.13 = (bf16[272,512]{1,0:T(8,128)(2,1)S(1)}, bf16[272,512]{1,0:T(8,128)(2,1)S(1)}, u32[]{:S(2)}, u32[]{:S(2)}) collective-permute-start(bf16[272,512]{1,0:T(8,128)(2,1)S(1)} %maximum_maximum_fusion.refs_3_), channel_id=1, source_target_pairs={{0,2},{1,3},{2,4},{3,5},{4,6},{5,7},{6,0},{7,1},{8,10},{9,11},{10,... | collective-permute-start | bytes 835592 | tf_op jit(solution)/shard_map/ppermute | solution.py:217
  10.9 11.3 %collective-permute-start.12 = (bf16[256,512]{1,0:T(8,128)(2,1)}, bf16[256,512]{1,0:T(8,128)(2,1)S(1)}, u32[]{:S(2)}, u32[]{:S(2)}) collective-permute-start(bf16[256,512]{1,0:T(8,128)(2,1)} %refs_2_.5), channel_id=1, source_target_pairs={{0,1},{1,0},{2,3},{3,2},{4,5},{5,4},{6,7},{7,6},{8,9},{9,8},{10,11... | collective-permute-start | bytes 786440 | tf_op jit(solution)/shard_map/ppermute | solution.py:217
  11.4 16.3 %collective-permute-start.1 = (bf16[256,512]{1,0:T(8,128)(2,1)S(1)}, bf16[256,512]{1,0:T(8,128)(2,1)S(1)}, u32[]{:S(2)}, u32[]{:S(2)}) collective-permute-start(bf16[256,512]{1,0:T(8,128)(2,1)S(1)} %collective-permute-done.refs_4_.refs_8_), channel_id=1, source_target_pairs={{0,1},{1,0},{2,3},{3,2},{4,5},{5,4},{6,7},{7,6},{8,9},{9,8},{10,11... | collective-permute-start | bytes 786440 | tf_op jit(solution)/shard_map/ppermute | solution.py:217
  22.1 22.5 %collective-permute-start.6 = (bf16[256,512]{1,0:T(8,128)(2,1)S(1)}, bf16[256,512]{1,0:T(8,128)(2,1)S(1)}, u32[]{:S(2)}, u32[]{:S(2)}) collective-permute-start(bf16[256,512]{1,0:T(8,128)(2,1)S(1)} %collective-permute-done.refs_4_.refs_8_), channel_id=1, source_target_pairs={{0,2},{1,3},{2,4},{3,5},{4,6},{5,7},{6,0},{7,1},{8,10},{9,11},{10,... | collective-permute-start | bytes 786440 | tf_op jit(solution)/shard_map/ppermute | solution.py:217
  22.5 25.6 %collective-permute-start.8 = (bf16[256,512]{1,0:T(8,128)(2,1)S(1)}, bf16[256,512]{1,0:T(8,128)(2,1)S(1)}, u32[]{:S(2)}, u32[]{:S(2)}) collective-permute-start(bf16[256,512]{1,0:T(8,128)(2,1)S(1)} %collective-permute-done.7.refs_5_.refs_9_), channel_id=1, source_target_pairs={{0,1},{1,0},{2,3},{3,2},{4,5},{5,4},{6,7},{7,6},{8,9},{9,8},{10,11... | collective-permute-start | bytes 786440 | tf_op jit(solution)/shard_map/ppermute | solution.py:217
  24.4 20.4 %collective-permute-start.4 = (bf16[272,512]{1,0:T(8,128)(2,1)S(1)}, bf16[272,512]{1,0:T(8,128)(2,1)S(1)}, u32[]{:S(2)}, u32[]{:S(2)}) collective-permute-start(bf16[272,512]{1,0:T(8,128)(2,1)S(1)} %collective-permute-done.3.refs_9_.refs_16_), channel_id=1, source_target_pairs={{0,6},{1,7},{2,0},{3,1},{4,2},{5,3},{6,4},{7,5},{8,14},{9,15},{10,... | collective-permute-start | bytes 835592 | tf_op jit(solution)/shard_map/ppermute | solution.py:217
  27.3 20.8 %collective-permute-start.11 = (bf16[272,512]{1,0:T(8,128)(2,1)S(1)}, bf16[272,512]{1,0:T(8,128)(2,1)S(1)}, u32[]{:S(2)}, u32[]{:S(2)}) collective-permute-start(bf16[272,512]{1,0:T(8,128)(2,1)S(1)} %collective-permute-done.3.refs_9_.refs_16_), channel_id=1, source_target_pairs={{0,2},{1,3},{2,4},{3,5},{4,6},{5,7},{6,0},{7,1},{8,10},{9,11},{10,... | collective-permute-start | bytes 835592 | tf_op jit(solution)/shard_map/ppermute | solution.py:217
  27.8 20.4 %collective-permute-start.10 = (bf16[272,512]{1,0:T(8,128)(2,1)S(1)}, bf16[272,512]{1,0:T(8,128)(2,1)S(1)}, u32[]{:S(2)}, u32[]{:S(2)}) collective-permute-start(bf16[272,512]{1,0:T(8,128)(2,1)S(1)} %collective-permute-done.9.refs_8_.refs_15_), channel_id=1, source_target_pairs={{0,6},{1,7},{2,0},{3,1},{4,2},{5,3},{6,4},{7,5},{8,14},{9,15},{10,... | collective-permute-start | bytes 835592 | tf_op jit(solution)/shard_map/ppermute | solution.py:217
  30.6 1.6 %copy-start = (bf16[256,4096]{1,0:T(8,128)(2,1)S(1)}, bf16[256,4096]{1,0:T(8,128)(2,1)}, u32[]{:S(2)}) copy-start(bf16[256,4096]{1,0:T(8,128)(2,1)} %refs_1_.5) | copy-start | bytes 6291460
  32.1 0.9 %copy-start.2 = (bf16[256,512]{1,0:T(8,128)(2,1)S(1)}, bf16[256,512]{1,0:T(8,128)(2,1)}, u32[]{:S(2)}) copy-start(bf16[256,512]{1,0:T(8,128)(2,1)} %refs_2_.5) | copy-start | bytes 786436
  33.1 15.0 %copy-start.1 = (bf16[256,4096]{1,0:T(8,128)(2,1)S(1)}, bf16[256,4096]{1,0:T(8,128)(2,1)}, u32[]{:S(2)}) copy-start(bf16[256,4096]{1,0:T(8,128)(2,1)} %refs_1_.5) | copy-start | bytes 6291460
  33.1 15.0 %copy-start.3 = (bf16[256,512]{1,0:T(8,128)(2,1)S(1)}, bf16[256,512]{1,0:T(8,128)(2,1)}, u32[]{:S(2)}) copy-start(bf16[256,512]{1,0:T(8,128)(2,1)} %refs_2_.5) | copy-start | bytes 786436
  44.6 13.1 %collective-permute-start.2 = (bf16[256,512]{1,0:T(8,128)(2,1)S(1)}, bf16[256,512]{1,0:T(8,128)(2,1)S(1)}, u32[]{:S(2)}, u32[]{:S(2)}) collective-permute-start(bf16[256,512]{1,0:T(8,128)(2,1)S(1)} %collective-permute-done.1.refs_5_.refs_12_), channel_id=1, source_target_pairs={{0,2},{1,3},{2,4},{3,5},{4,6},{5,7},{6,0},{7,1},{8,10},{9,11},{10,... | collective-permute-start | bytes 786440 | tf_op jit(solution)/shard_map/ppermute | solution.py:217
  44.9 12.8 %collective-permute-start.5 = (bf16[272,512]{1,0:T(8,128)(2,1)S(1)}, bf16[272,512]{1,0:T(8,128)(2,1)S(1)}, u32[]{:S(2)}, u32[]{:S(2)}) collective-permute-start(bf16[272,512]{1,0:T(8,128)(2,1)S(1)} %collective-permute-done.4.refs_9_.refs_19_), channel_id=1, source_target_pairs={{0,6},{1,7},{2,0},{3,1},{4,2},{5,3},{6,4},{7,5},{8,14},{9,15},{10,... | collective-permute-start | bytes 835592 | tf_op jit(solution)/shard_map/ppermute | solution.py:217
